TPU v7x, 32 devices: a whole 2x2x4 slice. The times are simulated.
32 devices in a mesh: blk: 8 (over z, x), rep: 4 (over y, core).
Axes of the slice: x: 2, y: 2, z: 4, core: 2. Of those that a mesh axis runs over, the one named last changes fastest.
Arguments:
- pixel_factors: float32 [24576, 256], P(('blk', 'rep')), may hold values from -1.5 to 1.5
- scene_factors: float32 [8192, 256], P('blk'), may hold values from -1.5 to 1.5
- elevations: bfloat16 [3, 24576, 1024], P(None, ('blk', 'rep')), may hold values from -6 to 6
- quality: bfloat16 [3, 24576, 1024], P(None, ('blk', 'rep')), may hold values from 0 to 1, as said below
- occupancy: int32 [3, 32], P(None, ('blk', 'rep')), may hold values from 0 to 1, as said below
Outputs:
- pixel_out: float32 [24576, 256], P(('blk', 'rep'))
- scene_out: float32 [8192, 256], P('blk')
Inputs may be any that keep to these rules, and one draw needn't show every extreme that they name: quality is zero on every entry of an owner's tile whose occupancy is 0; otherwise about half of the entries are nonzero. occupancy is 0 or 1 and about three quarters of the tiles are occupied.
All inputs are finite; a program needn't handle non-finite values.
Results may differ from a plain program's by a relative error of at most 0.0003.
Values sent between devices are 32-bit elements; how exact they have to be, the bound alone decides.
A program may use at most 64 MiB of HBM per device.

v0:
```python
import functools

import jax
import jax.numpy as jnp
from jax import lax
from jax.experimental import pallas as pl
from jax.experimental.pallas import tpu as pltpu
from jax.sharding import PartitionSpec as P

MESH = pl.DeviceIdType.MESH
STEPS = 3
CHUNK = 128
PAIR = 256
ROWS = 256
BAND = 128
VMEM_BYTES = 62 * 1024 * 1024
LAG_SUM = 1
LAG_UPDATE = 3
LAG_FORWARD = 6


def split(value):
    high = value.astype(jnp.bfloat16)
    return high, (value - high.astype(jnp.float32)).astype(jnp.bfloat16)


def dot(left, right):
    return jnp.dot(left, right, preferred_element_type=jnp.float32)


def kernel(
    blk_count, rep_count,
    occ_ref, pix_ref, scene_ref, elev_ref, qual_ref, pix_out, scene_out,
    elev, qual, u_ref, u_parts, ut_parts, v_first, v_all, v_high, v_low, m_high, m_low,
    grad, core_in, chip_sum, fresh,
    load_sem, first_sem, tile_sem, send_sem, core_recv, chip_recv, move_recv, fwd_recv,
):
    pixels, rank = pix_ref.shape
    acq = scene_ref.shape[0]
    per_step = acq // CHUNK
    total = STEPS * per_step
    half = rank // 2
    chips = rep_count // 2
    pixel_rate = 8.0 / acq
    scene_rate = 8.0 / (pixels * rep_count)

    group = lax.axis_index("blk")
    rep = lax.axis_index("rep")
    core = lax.rem(rep, 2)
    chip = lax.div(rep, 2)
    other_core = chip * 2 + 1 - core

    def at_blk(shift):
        return lax.rem(group + shift + blk_count, blk_count)

    barrier = pltpu.get_barrier_semaphore()
    partners = [(group, other_core)]
    for offset in range(1, chips):
        partners.append((group, lax.rem(chip + offset, chips) * 2 + core))
    for shift in (-1, 1, STEPS - 1, 1 - STEPS):
        partners.append((at_blk(shift), rep))
    for partner in partners:
        pl.semaphore_signal(barrier, inc=1, device_id=partner, device_id_type=MESH)

    load_u = pltpu.make_async_copy(pix_ref, u_ref, load_sem.at[0])
    load_u.start()

    def first_loads(c):
        cols = pl.ds(pl.multiple_of(c * CHUNK, CHUNK), CHUNK)
        return (
            pltpu.make_async_copy(scene_ref.at[cols], v_first.at[cols], first_sem.at[0, c]),
            pltpu.make_async_copy(elev_ref.at[0, :, cols], elev.at[0, :, cols], first_sem.at[1, c]),
            pltpu.make_async_copy(qual_ref.at[0, :, cols], qual.at[0, :, cols], first_sem.at[2, c]),
        )

    for c in range(per_step):
        for load in first_loads(c):
            load.start()

    def tile_loads(step):
        return (
            pltpu.make_async_copy(elev_ref.at[step], elev.at[step], tile_sem.at[0, step]),
            pltpu.make_async_copy(qual_ref.at[step], qual.at[step], tile_sem.at[1, step]),
        )


    load_u.wait()

    def core_copy(n):
        return pltpu.make_async_remote_copy(
            src_ref=grad.at[n, pl.ds(pl.multiple_of((1 - core) * half, half), half)],
            dst_ref=core_in.at[n],
            send_sem=send_sem.at[0], recv_sem=core_recv.at[n],
            device_id=(group, other_core), device_id_type=MESH,
        )

    def chip_copy(n, offset):
        return pltpu.make_async_remote_copy(
            src_ref=chip_sum.at[n, chip], dst_ref=chip_sum.at[n, chip],
            send_sem=send_sem.at[2 + offset], recv_sem=chip_recv.at[n, chip],
            device_id=(group, lax.rem(chip + offset, chips) * 2 + core), device_id_type=MESH,
        )

    def chip_arrival(n, offset):
        sender = lax.rem(chip + offset, chips)
        return pltpu.make_async_remote_copy(
            src_ref=chip_sum.at[n, sender], dst_ref=chip_sum.at[n, sender],
            send_sem=send_sem.at[2 + offset], recv_sem=chip_recv.at[n, sender],
            device_id=(group, sender * 2 + core), device_id_type=MESH,
        )

    def place(n, side):
        step = lax.div(n, per_step)
        return v_all.at[step + 1, lax.rem(n, per_step), pl.ds(pl.multiple_of(side * half, half), half)]

    def move_copy(n):
        last = lax.div(lax.div(n, per_step), STEPS - 1)
        return pltpu.make_async_remote_copy(
            src_ref=fresh.at[n], dst_ref=place(n, core),
            send_sem=send_sem.at[1], recv_sem=move_recv.at[n],
            device_id=(at_blk(last * STEPS - 1), rep), device_id_type=MESH,
        )

    def forward_copy(n):
        return pltpu.make_async_remote_copy(
            src_ref=place(n, core), dst_ref=place(n, core),
            send_sem=send_sem.at[2], recv_sem=fwd_recv.at[n],
            device_id=(group, other_core), device_id_type=MESH,
        )

    def forward_arrival(n):
        return pltpu.make_async_remote_copy(
            src_ref=place(n, 1 - core), dst_ref=place(n, 1 - core),
            send_sem=send_sem.at[2], recv_sem=fwd_recv.at[n],
            device_id=(group, other_core), device_id_type=MESH,
        )

    def begin_step(step):
        @pl.when(step > 0)
        def _():
            for load in tile_loads(step):
                load.wait()

        @pl.when(step + 1 < STEPS)
        def _():
            for load in tile_loads(step + 1):
                load.start()

        for start in range(0, pixels, ROWS):
            rows = pl.ds(start, ROWS)
            u = u_ref[rows, :]
            high, low = split(u)
            u_parts[0, rows, :] = high
            u_parts[1, rows, :] = low
            high, low = split(u.T)
            ut_parts[pl.ds(0, rank), rows] = high
            ut_parts[pl.ds(rank, rank), rows] = low

    def work(n):
        step = lax.div(n, per_step)
        first = pl.multiple_of(lax.rem(n, per_step) * CHUNK, CHUNK)
        cols = pl.ds(first, CHUNK)
        flag = occ_ref[0, step].astype(jnp.float32)
        v = v_all[step, lax.rem(n, per_step)]
        high, low = split(v.T)
        v_high[cols, :] = high
        v_low[cols, :] = low
        high, low = split(v)
        v_cat = jnp.concatenate([high, low], axis=1)
        for start in range(0, pixels, ROWS):
            rows = pl.ds(start, ROWS)
            by_high = dot(u_parts[0, rows, :], v_cat)
            by_low = dot(u_parts[1, rows, :], v_cat)
            predicted = by_high[:, :CHUNK] + (by_high[:, CHUNK:] + by_low[:, :CHUNK] + by_low[:, CHUNK:])
            weight = qual[step, rows, cols].astype(jnp.float32) * flag
            misfit = weight * (elev[step, rows, cols].astype(jnp.float32) - predicted)
            high, low = split(misfit)
            m_high[rows, cols] = high
            m_low[rows, cols] = low
        parts = dot(ut_parts[...], jnp.concatenate([m_high[:, cols], m_low[:, cols]], axis=1))
        by_high, by_low = parts[:rank], parts[rank:]
        grad[n] = by_high[:, :CHUNK] + (by_high[:, CHUNK:] + by_low[:, :CHUNK] + by_low[:, CHUNK:])

    def add_pixel_grad(n, begin, count):
        first = pl.multiple_of(lax.rem(n, per_step) * CHUNK + CHUNK - PAIR, PAIR)
        cols = pl.ds(first, PAIR)
        high, low = v_high[cols, :], v_low[cols, :]
        v_cat = jnp.concatenate([high, high, low], axis=0)
        for start in range(0, count, BAND):
            rows = pl.ds(pl.multiple_of(begin + start, BAND), BAND)
            high, low = m_high[rows, cols], m_low[rows, cols]
            u_ref[rows, :] += pixel_rate * dot(jnp.concatenate([high, low, high], axis=1), v_cat)

    def serve(t):
        n_sum = t - LAG_SUM

        @pl.when(jnp.logical_and(n_sum >= 0, n_sum < total))
        def _():
            core_copy(n_sum).wait_recv()
            own = grad[n_sum, pl.ds(pl.multiple_of(core * half, half), half), :]
            chip_sum[n_sum, chip] = own + core_in[n_sum]
            for offset in range(1, chips):
                chip_copy(n_sum, offset).start()

        n_new = t - LAG_UPDATE

        @pl.when(jnp.logical_and(n_new >= 0, n_new < total))
        def _():
            for offset in range(1, chips):
                chip_arrival(n_new, offset).wait_recv()
            summed = chip_sum[n_new, 0]
            for index in range(1, chips):
                summed = summed + chip_sum[n_new, index]
            old = v_all[lax.div(n_new, per_step), lax.rem(n_new, per_step), pl.ds(pl.multiple_of(core * half, half), half)]
            fresh[n_new] = old + scene_rate * summed
            move_copy(n_new).start()

        n_fwd = t - LAG_FORWARD

        @pl.when(n_fwd >= 0)
        def _():
            move_copy(n_fwd).wait_recv()
            forward_copy(n_fwd).start()

    pair = PAIR // CHUNK
    part = pixels // pair

    def take_first(c):
        for load in first_loads(c):
            load.wait()
        v_all[0, c] = v_first[pl.ds(pl.multiple_of(c * CHUNK, CHUNK), CHUNK), :].T

    def tick(t, carry):
        place_in_step = lax.rem(t, per_step)

        @pl.when(place_in_step == 0)
        def _():
            add_pixel_grad(t - 1, 0, pixels)
            begin_step(lax.div(t, per_step))

        @pl.when(t < per_step)
        def _():
            take_first(t)

        @pl.when(t >= per_step)
        def _():
            forward_arrival(t - per_step).wait_recv()

        @pl.when(place_in_step < pair)
        def _():
            work(t)

        @pl.when(place_in_step >= pair)
        def _():
            turn = lax.rem(place_in_step, pair)
            work(t)
            add_pixel_grad(t - turn - 1, turn * part, part)

        core_copy(t).start()
        serve(t)
        return carry

    def late_tick(t, carry):
        serve(t)
        return carry

    begin_step(0)
    take_first(0)
    work(0)
    pl.semaphore_wait(barrier, len(partners))
    core_copy(0).start()
    lax.fori_loop(1, total, tick, 0)

    add_pixel_grad(total - 1, 0, pixels)
    for start in range(0, pixels, ROWS):
        rows = pl.ds(start, ROWS)
        pix_out[rows, :] = u_ref[rows, :]
    lax.fori_loop(total, total + LAG_FORWARD, late_tick, 0)

    def finish(c, carry):
        forward_arrival((STEPS - 1) * per_step + c).wait_recv()
        cols = pl.ds(pl.multiple_of(c * CHUNK, CHUNK), CHUNK)
        scene_out[cols, :] = v_all[STEPS, c].T
        return carry

    lax.fori_loop(0, per_step, finish, 0)
    whole = [core_in, fresh, fresh] + [core_in] * (chips - 1)
    for index, like in enumerate(whole):
        pltpu.make_async_copy(like, like, send_sem.at[index]).wait()


def per_device(blk_count, rep_count, pixel_factors, scene_factors, elevations, quality, occupancy):
    pixels, rank = pixel_factors.shape
    acq = scene_factors.shape[0]
    total = STEPS * (acq // CHUNK)
    half = rank // 2
    chips = rep_count // 2
    f32, bf16 = jnp.float32, jnp.bfloat16
    in_vmem = pl.BlockSpec(memory_space=pltpu.VMEM)
    anywhere = pl.BlockSpec(memory_space=pl.ANY)
    dma = pltpu.SemaphoreType.DMA
    return pl.pallas_call(
        functools.partial(kernel, blk_count, rep_count),
        out_shape=(
            pltpu.VMEM((pixels, rank), f32),
            pltpu.VMEM((acq, rank), f32),
        ),
        in_specs=[pl.BlockSpec(memory_space=pltpu.SMEM)] + [anywhere] * 4,
        out_specs=(in_vmem, in_vmem),
        scratch_shapes=[
            pltpu.VMEM(elevations.shape, bf16),
            pltpu.VMEM(quality.shape, bf16),
            pltpu.VMEM((pixels, rank), f32),
            pltpu.VMEM((2, pixels, rank), bf16),
            pltpu.VMEM((2 * rank, pixels), bf16),
            pltpu.VMEM((acq, rank), f32),
            pltpu.VMEM((STEPS + 1, acq // CHUNK, rank, CHUNK), f32),
            pltpu.VMEM((acq, rank), bf16),
            pltpu.VMEM((acq, rank), bf16),
            pltpu.VMEM((pixels, acq), bf16),
            pltpu.VMEM((pixels, acq), bf16),
            pltpu.VMEM((total, rank, CHUNK), f32),
            pltpu.VMEM((total, half, CHUNK), f32),
            pltpu.VMEM((total, chips, half, CHUNK), f32),
            pltpu.VMEM((total, half, CHUNK), f32),
            dma((1,)),
            dma((3, acq // CHUNK)),
            dma((2, STEPS)),
            dma((2 + chips,)),
            dma((total,)),
            dma((total, chips)),
            dma((total,)),
            dma((total,)),
        ],
        compiler_params=pltpu.CompilerParams(
            collective_id=0, has_side_effects=True, vmem_limit_bytes=VMEM_BYTES
        ),
        cost_estimate=pl.CostEstimate(
            flops=18 * STEPS * pixels * acq * rank, bytes_accessed=12 * 1024 * 1024, transcendentals=0
        ),
    )(occupancy.T, pixel_factors, scene_factors, elevations, quality)


def solution(mesh):
    in_specs = (
        P(("blk", "rep"), None),
        P("blk", None),
        P(None, ("blk", "rep"), None),
        P(None, ("blk", "rep"), None),
        P(None, ("blk", "rep")),
    )
    out_specs = (P(("blk", "rep"), None), P("blk", None))
    return jax.shard_map(
        functools.partial(per_device, mesh.shape["blk"], mesh.shape["rep"]),
        mesh=mesh, in_specs=in_specs, out_specs=out_specs, check_vma=False,
    )
```

profile of v0, /device:TPU:1, one launch (start us, length us, event | category | flops | bytes accessed | tf_op | source)
XLA Modules:
  0.0 56.9 jit_solution(9649342138286604858)
XLA Ops:
  0.6 54.4 %shard_map.68 = (f32[768,256]{1,0:T(8,128)S(1)}, f32[1024,256]{1,0:T(8,128)S(1)}) custom-call(s32[1,3]{1,0:T(1,128)} %bitcast.1, f32[768,256]{1,0:T(8,128)} %pix_ref.1, f32[1024,256]{1,0:T(8,128)} %scene_ref.1, bf16[3,768,1024]{2,1,0:T(8,128)(2,1)} %elev_ref.1, bf16[3,768,1024]{2,1,0:T(8,128)(2,1)} %qual_ref.1), custom_call_target="tpu_custom_call" | custom-call | flops 10871635968 | bytes 12582912 | tf_op jit(solution)/shard_map/pallas_call | solution.py:302
  55.1 0.9 %copy.9 = f32[768,256]{1,0:T(8,128)} copy(f32[768,256]{1,0:T(8,128)S(1)} %get-tuple-element.2) | data formatting | bytes 1572864
  55.9 1.0 %copy.10 = f32[1024,256]{1,0:T(8,128)} copy(f32[1024,256]{1,0:T(8,128)S(1)} %get-tuple-element.3) | data formatting | bytes 2097152
where the time goes:
time: 57.1 us; the launch traced here: 56.9 us
  Pallas kernels  54.4 us (95%)
  local copies, waits for them, and re-layouts  1.85 us (3%)
  between operations  0.64 us (1%)
    pallas_call x1, Pallas kernels, per_device(): pl.pallas_call(functools.partial(kernel, blk_count, rep_count), out_shape...  54.4 us
    unnamed x2, local copies, waits for them, and re-layouts  1.85 us

commit v1 on v0

--- a/solution.py
+++ b/solution.py
@@ -14,7 +14,6 @@
 ROWS = 256
 BAND = 128
 VMEM_BYTES = 62 * 1024 * 1024
-LAG_SUM = 1
 LAG_UPDATE = 3
 LAG_FORWARD = 6
 
@@ -156,7 +155,7 @@
             ut_parts[pl.ds(0, rank), rows] = high
             ut_parts[pl.ds(rank, rank), rows] = low
 
-    def work(n):
+    def misfits(n):
         step = lax.div(n, per_step)
         first = pl.multiple_of(lax.rem(n, per_step) * CHUNK, CHUNK)
         cols = pl.ds(first, CHUNK)
@@ -177,6 +176,9 @@
             high, low = split(misfit)
             m_high[rows, cols] = high
             m_low[rows, cols] = low
+
+    def scene_grad(n):
+        cols = pl.ds(pl.multiple_of(lax.rem(n, per_step) * CHUNK, CHUNK), CHUNK)
         parts = dot(ut_parts[...], jnp.concatenate([m_high[:, cols], m_low[:, cols]], axis=1))
         by_high, by_low = parts[:rank], parts[rank:]
         grad[n] = by_high[:, :CHUNK] + (by_high[:, CHUNK:] + by_low[:, :CHUNK] + by_low[:, CHUNK:])
@@ -191,36 +193,31 @@
             high, low = m_high[rows, cols], m_low[rows, cols]
             u_ref[rows, :] += pixel_rate * dot(jnp.concatenate([high, low, high], axis=1), v_cat)
 
-    def serve(t):
-        n_sum = t - LAG_SUM
-
-        @pl.when(jnp.logical_and(n_sum >= 0, n_sum < total))
-        def _():
-            core_copy(n_sum).wait_recv()
-            own = grad[n_sum, pl.ds(pl.multiple_of(core * half, half), half), :]
-            chip_sum[n_sum, chip] = own + core_in[n_sum]
-            for offset in range(1, chips):
-                chip_copy(n_sum, offset).start()
-
-        n_new = t - LAG_UPDATE
-
-        @pl.when(jnp.logical_and(n_new >= 0, n_new < total))
-        def _():
-            for offset in range(1, chips):
-                chip_arrival(n_new, offset).wait_recv()
-            summed = chip_sum[n_new, 0]
-            for index in range(1, chips):
-                summed = summed + chip_sum[n_new, index]
-            old = v_all[lax.div(n_new, per_step), lax.rem(n_new, per_step), pl.ds(pl.multiple_of(core * half, half), half)]
-            fresh[n_new] = old + scene_rate * summed
-            move_copy(n_new).start()
-
-        n_fwd = t - LAG_FORWARD
-
-        @pl.when(n_fwd >= 0)
-        def _():
-            move_copy(n_fwd).wait_recv()
-            forward_copy(n_fwd).start()
+    def stage(n, body):
+        @pl.when(jnp.logical_and(n >= 0, n < total))
+        def _():
+            body(n)
+
+    def add_cores(n):
+        core_copy(n).wait_recv()
+        own = grad[n, pl.ds(pl.multiple_of(core * half, half), half), :]
+        chip_sum[n, chip] = own + core_in[n]
+        for offset in range(1, chips):
+            chip_copy(n, offset).start()
+
+    def update(n):
+        for offset in range(1, chips):
+            chip_arrival(n, offset).wait_recv()
+        summed = chip_sum[n, 0]
+        for index in range(1, chips):
+            summed = summed + chip_sum[n, index]
+        old = v_all[lax.div(n, per_step), lax.rem(n, per_step), pl.ds(pl.multiple_of(core * half, half), half)]
+        fresh[n] = old + scene_rate * summed
+        move_copy(n).start()
+
+    def forward(n):
+        move_copy(n).wait_recv()
+        forward_copy(n).start()
 
     pair = PAIR // CHUNK
     part = pixels // pair
@@ -236,6 +233,7 @@
         @pl.when(place_in_step == 0)
         def _():
             add_pixel_grad(t - 1, 0, pixels)
+            add_cores(t - 1)
             begin_step(lax.div(t, per_step))
 
         @pl.when(t < per_step)
@@ -248,30 +246,39 @@
 
         @pl.when(place_in_step < pair)
         def _():
-            work(t)
+            misfits(t)
 
         @pl.when(place_in_step >= pair)
         def _():
             turn = lax.rem(place_in_step, pair)
-            work(t)
+            misfits(t)
             add_pixel_grad(t - turn - 1, turn * part, part)
 
+        @pl.when(place_in_step != 0)
+        def _():
+            add_cores(t - 1)
+
+        stage(t - LAG_FORWARD, forward)
+        scene_grad(t)
         core_copy(t).start()
-        serve(t)
+        stage(t - LAG_UPDATE, update)
         return carry
 
     def late_tick(t, carry):
-        serve(t)
+        stage(t - LAG_UPDATE, update)
+        stage(t - LAG_FORWARD, forward)
         return carry
 
     begin_step(0)
     take_first(0)
-    work(0)
+    misfits(0)
+    scene_grad(0)
     pl.semaphore_wait(barrier, len(partners))
     core_copy(0).start()
     lax.fori_loop(1, total, tick, 0)
 
     add_pixel_grad(total - 1, 0, pixels)
+    add_cores(total - 1)
     for start in range(0, pixels, ROWS):
         rows = pl.ds(start, ROWS)
         pix_out[rows, :] = u_ref[rows, :]

time: 57.1 us -> 57 us (level)
  no operation moved by 1% of the time
where the time goes in v1:
time: 57 us; the launch traced here: 56.9 us
  Pallas kernels  54.4 us (95%)
  local copies, waits for them, and re-layouts  1.85 us (3%)
  between operations  0.64 us (1%)
    pallas_call x1, Pallas kernels, per_device(): pl.pallas_call(functools.partial(kernel, blk_count, rep_count), out_shape...  54.4 us
    unnamed x2, local copies, waits for them, and re-layouts  1.85 us

profile of v1, /device:TPU:1, one launch (start us, length us, event | category | flops | bytes accessed | tf_op | source)
XLA Modules:
  0.0 56.9 jit_solution(6031597657456028621)
XLA Ops:
  0.6 54.4 %shard_map.68 = (f32[768,256]{1,0:T(8,128)S(1)}, f32[1024,256]{1,0:T(8,128)S(1)}) custom-call(s32[1,3]{1,0:T(1,128)} %bitcast.1, f32[768,256]{1,0:T(8,128)} %pix_ref.1, f32[1024,256]{1,0:T(8,128)} %scene_ref.1, bf16[3,768,1024]{2,1,0:T(8,128)(2,1)} %elev_ref.1, bf16[3,768,1024]{2,1,0:T(8,128)(2,1)} %qual_ref.1), custom_call_target="tpu_custom_call" | custom-call | flops 10871635968 | bytes 12582912 | tf_op jit(solution)/shard_map/pallas_call | solution.py:309
  55.0 0.9 %copy.9 = f32[768,256]{1,0:T(8,128)} copy(f32[768,256]{1,0:T(8,128)S(1)} %get-tuple-element.2) | data formatting | bytes 1572864
  55.9 1.0 %copy.10 = f32[1024,256]{1,0:T(8,128)} copy(f32[1024,256]{1,0:T(8,128)S(1)} %get-tuple-element.3) | data formatting | bytes 2097152

commit v2 on v1

--- a/solution.py
+++ b/solution.py
@@ -12,7 +12,6 @@
 CHUNK = 128
 PAIR = 256
 ROWS = 256
-BAND = 128
 VMEM_BYTES = 62 * 1024 * 1024
 LAG_UPDATE = 3
 LAG_FORWARD = 6
@@ -149,11 +148,14 @@
             rows = pl.ds(start, ROWS)
             u = u_ref[rows, :]
             high, low = split(u)
-            u_parts[0, rows, :] = high
-            u_parts[1, rows, :] = low
+            u_parts[rows, :] = high
+            u_parts[pl.ds(pixels + start, ROWS), :] = low
             high, low = split(u.T)
             ut_parts[pl.ds(0, rank), rows] = high
             ut_parts[pl.ds(rank, rank), rows] = low
+
+    pair = PAIR // CHUNK
+    part = pixels // pair
 
     def misfits(n):
         step = lax.div(n, per_step)
@@ -166,10 +168,11 @@
         v_low[cols, :] = low
         high, low = split(v)
         v_cat = jnp.concatenate([high, low], axis=1)
+        products = dot(u_parts[...], v_cat)
         for start in range(0, pixels, ROWS):
             rows = pl.ds(start, ROWS)
-            by_high = dot(u_parts[0, rows, :], v_cat)
-            by_low = dot(u_parts[1, rows, :], v_cat)
+            by_high = products[start : start + ROWS]
+            by_low = products[pixels + start : pixels + start + ROWS]
             predicted = by_high[:, :CHUNK] + (by_high[:, CHUNK:] + by_low[:, :CHUNK] + by_low[:, CHUNK:])
             weight = qual[step, rows, cols].astype(jnp.float32) * flag
             misfit = weight * (elev[step, rows, cols].astype(jnp.float32) - predicted)
@@ -188,10 +191,9 @@
         cols = pl.ds(first, PAIR)
         high, low = v_high[cols, :], v_low[cols, :]
         v_cat = jnp.concatenate([high, high, low], axis=0)
-        for start in range(0, count, BAND):
-            rows = pl.ds(pl.multiple_of(begin + start, BAND), BAND)
-            high, low = m_high[rows, cols], m_low[rows, cols]
-            u_ref[rows, :] += pixel_rate * dot(jnp.concatenate([high, low, high], axis=1), v_cat)
+        rows = pl.ds(pl.multiple_of(begin, part), count)
+        high, low = m_high[rows, cols], m_low[rows, cols]
+        u_ref[rows, :] += pixel_rate * dot(jnp.concatenate([high, low, high], axis=1), v_cat)
 
     def stage(n, body):
         @pl.when(jnp.logical_and(n >= 0, n < total))
@@ -218,9 +220,6 @@
     def forward(n):
         move_copy(n).wait_recv()
         forward_copy(n).start()
-
-    pair = PAIR // CHUNK
-    part = pixels // pair
 
     def take_first(c):
         for load in first_loads(c):
@@ -318,7 +317,7 @@
             pltpu.VMEM(elevations.shape, bf16),
             pltpu.VMEM(quality.shape, bf16),
             pltpu.VMEM((pixels, rank), f32),
-            pltpu.VMEM((2, pixels, rank), bf16),
+            pltpu.VMEM((2 * pixels, rank), bf16),
             pltpu.VMEM((2 * rank, pixels), bf16),
             pltpu.VMEM((acq, rank), f32),
             pltpu.VMEM((STEPS + 1, acq // CHUNK, rank, CHUNK), f32),

time: 57 us -> 57.8 us (1.014)
  Pallas kernels: 54.4 us -> 55.1 us
    pallas_call x1, Pallas kernels: 54.4 us -> 55.1 us  [per_device(): pl.pallas_call(functools.partial(kernel, blk_count, rep_count), out_shape...]
where the time goes in v2:
time: 57.8 us; the launch traced here: 57.6 us
  Pallas kernels  55.1 us (95%)
  local copies, waits for them, and re-layouts  1.85 us (3%)
  between operations  0.64 us (1%)
    pallas_call x1, Pallas kernels, per_device(): pl.pallas_call(functools.partial(kernel, blk_count, rep_count), out_shape...  55.1 us
    unnamed x2, local copies, waits for them, and re-layouts  1.85 us

profile of v2, /device:TPU:1, one launch (start us, length us, event | category | flops | bytes accessed | tf_op | source)
XLA Modules:
  0.0 57.6 jit_solution(5355324344766594046)
XLA Ops:
  0.6 55.1 %shard_map.68 = (f32[768,256]{1,0:T(8,128)S(1)}, f32[1024,256]{1,0:T(8,128)S(1)}) custom-call(s32[1,3]{1,0:T(1,128)} %bitcast.1, f32[768,256]{1,0:T(8,128)} %pix_ref.1, f32[1024,256]{1,0:T(8,128)} %scene_ref.1, bf16[3,768,1024]{2,1,0:T(8,128)(2,1)} %elev_ref.1, bf16[3,768,1024]{2,1,0:T(8,128)(2,1)} %qual_ref.1), custom_call_target="tpu_custom_call" | custom-call | flops 10871635968 | bytes 12582912 | tf_op jit(solution)/shard_map/pallas_call | solution.py:308
  55.8 0.9 %copy.9 = f32[768,256]{1,0:T(8,128)} copy(f32[768,256]{1,0:T(8,128)S(1)} %get-tuple-element.2) | data formatting | bytes 1572864
  56.6 1.0 %copy.10 = f32[1024,256]{1,0:T(8,128)} copy(f32[1024,256]{1,0:T(8,128)S(1)} %get-tuple-element.3) | data formatting | bytes 2097152

commit v3 on v1

--- a/solution.py
+++ b/solution.py
@@ -14,7 +14,8 @@
 ROWS = 256
 BAND = 128
 VMEM_BYTES = 62 * 1024 * 1024
-LAG_UPDATE = 3
+LAG_UPDATE = 2
+LAG_SPREAD = 5
 LAG_FORWARD = 6
 
 
@@ -31,8 +32,8 @@
     blk_count, rep_count,
     occ_ref, pix_ref, scene_ref, elev_ref, qual_ref, pix_out, scene_out,
     elev, qual, u_ref, u_parts, ut_parts, v_first, v_all, v_high, v_low, m_high, m_low,
-    grad, core_in, chip_sum, fresh,
-    load_sem, first_sem, tile_sem, send_sem, core_recv, chip_recv, move_recv, fwd_recv,
+    grad, core_in, summed, chip_in, fresh,
+    load_sem, first_sem, tile_sem, send_sem, core_recv, chip_recv, spread_recv, move_recv, fwd_recv,
 ):
     pixels, rank = pix_ref.shape
     acq = scene_ref.shape[0]
@@ -40,6 +41,7 @@
     total = STEPS * per_step
     half = rank // 2
     chips = rep_count // 2
+    share = half // chips
     pixel_rate = 8.0 / acq
     scene_rate = 8.0 / (pixels * rep_count)
 
@@ -93,19 +95,40 @@
             device_id=(group, other_core), device_id_type=MESH,
         )
 
+    def peer(offset):
+        return lax.rem(chip + offset, chips)
+
     def chip_copy(n, offset):
-        return pltpu.make_async_remote_copy(
-            src_ref=chip_sum.at[n, chip], dst_ref=chip_sum.at[n, chip],
+        rows = pl.ds(pl.multiple_of(peer(offset) * share, share), share)
+        return pltpu.make_async_remote_copy(
+            src_ref=summed.at[n, rows], dst_ref=chip_in.at[n, chip],
             send_sem=send_sem.at[2 + offset], recv_sem=chip_recv.at[n, chip],
-            device_id=(group, lax.rem(chip + offset, chips) * 2 + core), device_id_type=MESH,
+            device_id=(group, peer(offset) * 2 + core), device_id_type=MESH,
         )
 
     def chip_arrival(n, offset):
-        sender = lax.rem(chip + offset, chips)
-        return pltpu.make_async_remote_copy(
-            src_ref=chip_sum.at[n, sender], dst_ref=chip_sum.at[n, sender],
-            send_sem=send_sem.at[2 + offset], recv_sem=chip_recv.at[n, sender],
-            device_id=(group, sender * 2 + core), device_id_type=MESH,
+        return pltpu.make_async_remote_copy(
+            src_ref=chip_in.at[n, peer(offset)], dst_ref=chip_in.at[n, peer(offset)],
+            send_sem=send_sem.at[2 + offset], recv_sem=chip_recv.at[n, peer(offset)],
+            device_id=(group, peer(offset) * 2 + core), device_id_type=MESH,
+        )
+
+    def part_place(n, owner):
+        start = core * half + owner * share
+        return v_all.at[lax.div(n, per_step) + 1, lax.rem(n, per_step), pl.ds(pl.multiple_of(start, share), share)]
+
+    def spread_copy(n, offset):
+        return pltpu.make_async_remote_copy(
+            src_ref=part_place(n, chip), dst_ref=part_place(n, chip),
+            send_sem=send_sem.at[1 + chips + offset], recv_sem=spread_recv.at[n, chip],
+            device_id=(group, peer(offset) * 2 + core), device_id_type=MESH,
+        )
+
+    def spread_arrival(n, offset):
+        return pltpu.make_async_remote_copy(
+            src_ref=part_place(n, peer(offset)), dst_ref=part_place(n, peer(offset)),
+            send_sem=send_sem.at[1 + chips + offset], recv_sem=spread_recv.at[n, peer(offset)],
+            device_id=(group, peer(offset) * 2 + core), device_id_type=MESH,
         )
 
     def place(n, side):
@@ -115,7 +138,7 @@
     def move_copy(n):
         last = lax.div(lax.div(n, per_step), STEPS - 1)
         return pltpu.make_async_remote_copy(
-            src_ref=fresh.at[n], dst_ref=place(n, core),
+            src_ref=fresh.at[n], dst_ref=part_place(n, chip),
             send_sem=send_sem.at[1], recv_sem=move_recv.at[n],
             device_id=(at_blk(last * STEPS - 1), rep), device_id_type=MESH,
         )
@@ -201,22 +224,30 @@
     def add_cores(n):
         core_copy(n).wait_recv()
         own = grad[n, pl.ds(pl.multiple_of(core * half, half), half), :]
-        chip_sum[n, chip] = own + core_in[n]
+        summed[n] = own + core_in[n]
         for offset in range(1, chips):
             chip_copy(n, offset).start()
 
     def update(n):
+        chip_in[n, chip] = summed[n, pl.ds(pl.multiple_of(chip * share, share), share), :]
         for offset in range(1, chips):
             chip_arrival(n, offset).wait_recv()
-        summed = chip_sum[n, 0]
+        gradient = chip_in[n, 0]
         for index in range(1, chips):
-            summed = summed + chip_sum[n, index]
-        old = v_all[lax.div(n, per_step), lax.rem(n, per_step), pl.ds(pl.multiple_of(core * half, half), half)]
-        fresh[n] = old + scene_rate * summed
+            gradient = gradient + chip_in[n, index]
+        start = core * half + chip * share
+        old = v_all[lax.div(n, per_step), lax.rem(n, per_step), pl.ds(pl.multiple_of(start, share), share)]
+        fresh[n] = old + scene_rate * gradient
         move_copy(n).start()
 
+    def spread(n):
+        move_copy(n).wait_recv()
+        for offset in range(1, chips):
+            spread_copy(n, offset).start()
+
     def forward(n):
-        move_copy(n).wait_recv()
+        for offset in range(1, chips):
+            spread_arrival(n, offset).wait_recv()
         forward_copy(n).start()
 
     pair = PAIR // CHUNK
@@ -258,14 +289,16 @@
         def _():
             add_cores(t - 1)
 
-        stage(t - LAG_FORWARD, forward)
+        stage(t - LAG_SPREAD, spread)
         scene_grad(t)
         core_copy(t).start()
         stage(t - LAG_UPDATE, update)
+        stage(t - LAG_FORWARD, forward)
         return carry
 
     def late_tick(t, carry):
         stage(t - LAG_UPDATE, update)
+        stage(t - LAG_SPREAD, spread)
         stage(t - LAG_FORWARD, forward)
         return carry
 
@@ -291,7 +324,7 @@
         return carry
 
     lax.fori_loop(0, per_step, finish, 0)
-    whole = [core_in, fresh, fresh] + [core_in] * (chips - 1)
+    whole = [core_in, fresh, core_in] + [fresh] * (2 * chips - 2)
     for index, like in enumerate(whole):
         pltpu.make_async_copy(like, like, send_sem.at[index]).wait()
 
@@ -302,6 +335,7 @@
     total = STEPS * (acq // CHUNK)
     half = rank // 2
     chips = rep_count // 2
+    share = half // chips
     f32, bf16 = jnp.float32, jnp.bfloat16
     in_vmem = pl.BlockSpec(memory_space=pltpu.VMEM)
     anywhere = pl.BlockSpec(memory_space=pl.ANY)
@@ -328,13 +362,15 @@
             pltpu.VMEM((pixels, acq), bf16),
             pltpu.VMEM((total, rank, CHUNK), f32),
             pltpu.VMEM((total, half, CHUNK), f32),
-            pltpu.VMEM((total, chips, half, CHUNK), f32),
             pltpu.VMEM((total, half, CHUNK), f32),
+            pltpu.VMEM((total, chips, half // chips, CHUNK), f32),
+            pltpu.VMEM((total, half // chips, CHUNK), f32),
             dma((1,)),
             dma((3, acq // CHUNK)),
             dma((2, STEPS)),
-            dma((2 + chips,)),
+            dma((1 + 2 * chips,)),
             dma((total,)),
+            dma((total, chips)),
             dma((total, chips)),
             dma((total,)),
             dma((total,)),

time: 57 us -> 69.8 us (1.22)
  Pallas kernels: 54.4 us -> 67.1 us
    pallas_call x1, Pallas kernels: 54.4 us -> 67.1 us  [per_device(): pl.pallas_call(functools.partial(kernel, blk_count, rep_count), out_shape...]
where the time goes in v3:
time: 69.8 us; the launch traced here: 69.6 us
  Pallas kernels  67.1 us (96%)
  local copies, waits for them, and re-layouts  1.85 us (3%)
    pallas_call x1, Pallas kernels, per_device(): pl.pallas_call(functools.partial(kernel, blk_count, rep_count), out_shape...  67.1 us
    unnamed x2, local copies, waits for them, and re-layouts  1.85 us

profile of v3, /device:TPU:1, one launch (start us, length us, event | category | flops | bytes accessed | tf_op | source)
XLA Modules:
  0.0 69.6 jit_solution(12993660820277784933)
XLA Ops:
  0.6 67.1 %shard_map.68 = (f32[768,256]{1,0:T(8,128)S(1)}, f32[1024,256]{1,0:T(8,128)S(1)}) custom-call(s32[1,3]{1,0:T(1,128)} %bitcast.1, f32[768,256]{1,0:T(8,128)} %pix_ref.1, f32[1024,256]{1,0:T(8,128)} %scene_ref.1, bf16[3,768,1024]{2,1,0:T(8,128)(2,1)} %elev_ref.1, bf16[3,768,1024]{2,1,0:T(8,128)(2,1)} %qual_ref.1), custom_call_target="tpu_custom_call" | custom-call | flops 10871635968 | bytes 12582912 | tf_op jit(solution)/shard_map/pallas_call | solution.py:343
  67.8 0.9 %copy.9 = f32[768,256]{1,0:T(8,128)} copy(f32[768,256]{1,0:T(8,128)S(1)} %get-tuple-element.2) | data formatting | bytes 1572864
  68.6 1.0 %copy.10 = f32[1024,256]{1,0:T(8,128)} copy(f32[1024,256]{1,0:T(8,128)S(1)} %get-tuple-element.3) | data formatting | bytes 2097152
